TPU v7x, 32 devices: a whole 2x2x4 slice. The times are simulated.
32 devices in a mesh: row: 16 (over z, x, core), col: 2 (over y).
Axes of the slice: x: 2, y: 2, z: 4, core: 2. Of those that a mesh axis runs over, the one named last changes fastest.
Arguments:
- matrix: float32 [4096, 1024], P('row', 'col'), may hold values from -12 to 12
Outputs:
- rotated: float32 [4096, 1024], P('row', 'col')
- coupling: float32 [2], replicated
All inputs are finite; a program needn't handle non-finite values.
Results may differ from a plain program's by a relative error of at most 0.00027.
Values sent between devices are 32-bit elements; how exact they have to be, the bound alone decides.
A program may use at most 64 MiB of HBM per device.

v0:
```python
import jax
import jax.numpy as jnp
from jax import lax
from jax.sharding import PartitionSpec as P

STEPS = 2


def from_behind(value, axis, steps):
    count = lax.axis_size(axis)
    first, last = (max(0, -steps), min(count, count - steps))
    return lax.ppermute(value, axis, [(source, source + steps) for source in range(first, last)])


def pair_grams(pair_blocks):
    return jnp.einsum(
        "prk,prl->pkl",
        pair_blocks,
        pair_blocks,
        precision=lax.Precision.HIGHEST,
        preferred_element_type=jnp.float32,
    )


def coupling_term(pair_gram, width):
    diagonal = jnp.diagonal(pair_gram, axis1=1, axis2=2)
    cross = pair_gram[:, :width, width:]
    return jnp.sum(cross * cross / (diagonal[:, :width, None] * diagonal[:, None, width:]))


def lower_solve(second, right_side):
    return jax.scipy.linalg.solve_triangular(second, right_side, lower=True)


def body(matrix):
    width = matrix.shape[1] // 2
    col_place = lax.axis_index("col")
    col_last = lax.axis_size("col") - 1
    first_col = col_place == 0
    last_col = col_place == col_last
    top_block = matrix[:, :width]
    bottom_block = matrix[:, width:]
    pair_blocks = matrix[None]
    pair_gram = lax.psum(pair_grams(pair_blocks), "row")
    coupling_terms = []
    for step_index in range(STEPS):
        local_term = coupling_term(pair_gram, width)
        coupling_terms.append(local_term)
        lower_factor = jnp.linalg.cholesky(pair_gram)
        inner_gram = jnp.einsum(
            "pik,pil->pkl",
            lower_factor,
            lower_factor,
            precision=lax.Precision.HIGHEST,
            preferred_element_type=jnp.float32,
        )
        second = jnp.linalg.cholesky(inner_gram)
        rotation = jnp.swapaxes(lower_solve(second, jnp.swapaxes(lower_factor, 1, 2)), 1, 2)
        turned = jnp.einsum(
            "prk,pkl->prl",
            pair_blocks,
            rotation,
            precision=lax.Precision.HIGHEST,
            preferred_element_type=jnp.float32,
        )
        new_top = turned[0, :, :width]
        new_bottom = turned[0, :, width:]
        outgoing = jnp.where(first_col, new_bottom, new_top)
        arrived_top = from_behind(outgoing, "col", 1)
        arrived_bottom = from_behind(new_bottom, "col", -1)
        top_block = jnp.where(first_col, new_top, arrived_top)
        bottom_block = jnp.where(last_col, new_top, arrived_bottom)
        pair_blocks = jnp.concatenate([top_block, bottom_block], axis=1)[None]
        if step_index + 1 < STEPS:
            pair_gram = lax.psum(pair_grams(pair_blocks), "row")
    totals = lax.psum(jnp.stack(coupling_terms), "col")
    coupling = jnp.sqrt(totals / (1.0 * lax.axis_size("col") * width))
    rotated = jnp.concatenate([top_block, bottom_block], axis=1)
    return (rotated, coupling)


def solution(mesh):
    in_specs = (P("row", "col"),)
    out_specs = (P("row", "col"), P())
    return jax.shard_map(body, mesh=mesh, in_specs=in_specs, out_specs=out_specs, check_vma=False)
```

profile of v0, /device:TPU:0, one launch (start us, length us, event | category | flops | bytes accessed | tf_op | source)
XLA Modules:
  0.0 741.8 jit_solution(16183585151848917020)
XLA Ops:
  8.2 2.1 convolution_bitcast_fusion.1
  10.4 97.2 %all-reduce.4.cloned.1.call-done = f32[1,512,512]{1,2,0:T(8,128)} async-done(((f32[1,512,512]{1,2,0:T(8,128)}), f32[1,512,512]{1,2,0:T(8,128)}) %all-reduce.4.cloned.1.call-update) | async-done | bytes 1048592 | tf_op jit(solution)/shard_map/psum | solution.py:44
  107.6 1.6 copy.14
  110.5 11.7 %custom-call.53 = f32[1,128,128]{2,1,0:T(8,128)S(1)} custom-call(f32[1,128,128]{2,1,0:T(8,128)S(1)} %cholesky.741), custom_call_target="Cholesky" | custom-call | tf_op jit(solution)/shard_map/jit(cholesky)/cholesky | solution.py:49
  122.2 9.8 %custom-call.54 = f32[1,1,128,128]{2,3,1,0:T(8,128)S(1)} custom-call(f32[1,1,128,128]{3,2,1,0:T(8,128)S(1)} %get-tuple-element.87), custom_call_target="InvertDiagBlocksLowerTriangular" | custom-call | tf_op jit(solution)/shard_map/jit(cholesky)/cholesky | solution.py:49
  134.7 11.7 %custom-call.55 = f32[1,128,128]{2,1,0:T(8,128)S(1)} custom-call(f32[1,128,128]{2,1,0:T(8,128)S(1)} %cholesky.745), custom_call_target="Cholesky" | custom-call | tf_op jit(solution)/shard_map/jit(cholesky)/cholesky | solution.py:49
  146.4 10.1 %custom-call.56 = f32[1,1,128,128]{2,3,1,0:T(8,128)S(1)} custom-call(f32[1,1,128,128]{3,2,1,0:T(8,128)S(1)} %get-tuple-element.84), custom_call_target="InvertDiagBlocksLowerTriangular" | custom-call | tf_op jit(solution)/shard_map/jit(cholesky)/cholesky | solution.py:49
  158.1 11.7 %custom-call.57 = f32[1,128,128]{2,1,0:T(8,128)S(1)} custom-call(f32[1,128,128]{2,1,0:T(8,128)S(1)} %cholesky.750), custom_call_target="Cholesky" | custom-call | tf_op jit(solution)/shard_map/jit(cholesky)/cholesky | solution.py:49
  170.6 9.8 %custom-call.58 = f32[1,1,128,128]{2,3,1,0:T(8,128)S(1)} custom-call(f32[1,1,128,128]{3,2,1,0:T(8,128)S(1)} %get-tuple-element.81), custom_call_target="InvertDiagBlocksLowerTriangular" | custom-call | tf_op jit(solution)/shard_map/jit(cholesky)/cholesky | solution.py:49
  181.8 11.7 %custom-call.59 = f32[1,128,128]{2,1,0:T(8,128)S(1)} custom-call(f32[1,128,128]{2,1,0:T(8,128)S(1)} %fusion.16), custom_call_target="Cholesky" | custom-call | tf_op jit(solution)/shard_map/jit(cholesky)/cholesky | solution.py:49
  198.9 2.9 fusion.39
  201.8 2.6 copy.16
  206.9 11.7 %custom-call.60 = f32[1,128,128]{2,1,0:T(8,128)S(1)} custom-call(f32[1,128,128]{2,1,0:T(8,128)S(1)} %cholesky.754), custom_call_target="Cholesky" | custom-call | tf_op jit(solution)/shard_map/jit(cholesky)/cholesky | solution.py:57
  219.3 9.8 %custom-call.61 = f32[1,1,128,128]{2,3,1,0:T(8,128)S(1)} custom-call(f32[1,1,128,128]{3,2,1,0:T(8,128)S(1)} %get-tuple-element.77), custom_call_target="InvertDiagBlocksLowerTriangular" | custom-call | tf_op jit(solution)/shard_map/jit(cholesky)/cholesky | solution.py:57
  231.8 11.9 %custom-call.62 = f32[1,128,128]{2,1,0:T(8,128)S(1)} custom-call(f32[1,128,128]{2,1,0:T(8,128)S(1)} %cholesky.758), custom_call_target="Cholesky" | custom-call | tf_op jit(solution)/shard_map/jit(cholesky)/cholesky | solution.py:57
  244.4 9.8 %custom-call.63 = f32[1,1,128,128]{2,3,1,0:T(8,128)S(1)} custom-call(f32[1,1,128,128]{3,2,1,0:T(8,128)S(1)} %get-tuple-element.74), custom_call_target="InvertDiagBlocksLowerTriangular" | custom-call | tf_op jit(solution)/shard_map/jit(cholesky)/cholesky | solution.py:57
  255.8 11.7 %custom-call.64 = f32[1,128,128]{2,1,0:T(8,128)S(1)} custom-call(f32[1,128,128]{2,1,0:T(8,128)S(1)} %cholesky.763), custom_call_target="Cholesky" | custom-call | tf_op jit(solution)/shard_map/jit(cholesky)/cholesky | solution.py:57
  268.2 9.8 %custom-call.65 = f32[1,1,128,128]{2,3,1,0:T(8,128)S(1)} custom-call(f32[1,1,128,128]{3,2,1,0:T(8,128)S(1)} %get-tuple-element.71), custom_call_target="InvertDiagBlocksLowerTriangular" | custom-call | tf_op jit(solution)/shard_map/jit(cholesky)/cholesky | solution.py:57
  279.4 12.1 %custom-call.66 = f32[1,128,128]{2,1,0:T(8,128)S(1)} custom-call(f32[1,128,128]{2,1,0:T(8,128)S(1)} %fusion.17), custom_call_target="Cholesky" | custom-call | tf_op jit(solution)/shard_map/jit(cholesky)/cholesky | solution.py:57
  295.9 11.6 %while.4 = (s32[]{:T(128)}, f32[512,512]{1,0:T(8,128)}, s32[4,2]{0,1:T(2,128)S(1)}, f32[4,128,128]{2,1,0:T(8,128)S(1)}, s32[]{:T(128)}) while((s32[]{:T(128)}, f32[512,512]{1,0:T(8,128)}, s32[4,2]{0,1:T(2,128)S(1)}, f32[4,128,128]{2,1,0:T(8,128)S(1)}, s32[]{:T(128)}) %tuple.75), condition=%wide.while_cond, body=%wide.while_body.sunk | while | flops 2 | bytes 131189 | solution.py:32
  296.6 2.3 bitcast_dynamic-update-slice_fusion.4
  299.5 2.3 bitcast_dynamic-update-slice_fusion.4
  302.4 2.3 bitcast_dynamic-update-slice_fusion.4
  305.3 2.2 bitcast_dynamic-update-slice_fusion.4
  307.5 39.3 %custom-call.67 = f32[4,128,128]{1,2,0:T(8,128)S(1)} custom-call(f32[4,128,128]{2,1,0:T(8,128)S(1)} %get-tuple-element.18), custom_call_target="InvertDiagBlocksLowerTriangular" | custom-call | tf_op jit(solution)/shard_map/jit(_solve_triangular)/triangular_solve | solution.py:32
  348.2 1.6 convolution_subtract_fusion.3
  350.3 1.9 convolution_subtract_fusion.2
  352.6 2.4 convolution_subtract_fusion.5
  356.5 3.4 collective-permute-start
  361.2 3.6 collective-permute-done
  364.8 4.1 collective-permute-done.1
  369.0 2.1 convolution_bitcast_fusion
  371.1 4.7 gather_fusion
  376.6 85.9 %all-reduce.6.cloned.1.call-done = f32[1,512,512]{1,2,0:T(8,128)} async-done(((f32[1,512,512]{1,2,0:T(8,128)}), f32[1,512,512]{1,2,0:T(8,128)}) %all-reduce.6.cloned.1.call-update) | async-done | bytes 1048592 | tf_op jit(solution)/shard_map/psum | solution.py:75
  462.5 1.6 copy.18
  465.4 11.7 %custom-call.68 = f32[1,128,128]{2,1,0:T(8,128)S(1)} custom-call(f32[1,128,128]{2,1,0:T(8,128)S(1)} %cholesky.767), custom_call_target="Cholesky" | custom-call | tf_op jit(solution)/shard_map/jit(cholesky)/cholesky | solution.py:49
  477.8 9.8 %custom-call.69 = f32[1,1,128,128]{2,3,1,0:T(8,128)S(1)} custom-call(f32[1,1,128,128]{3,2,1,0:T(8,128)S(1)} %get-tuple-element.67), custom_call_target="InvertDiagBlocksLowerTriangular" | custom-call | tf_op jit(solution)/shard_map/jit(cholesky)/cholesky | solution.py:49
  490.3 11.7 %custom-call.70 = f32[1,128,128]{2,1,0:T(8,128)S(1)} custom-call(f32[1,128,128]{2,1,0:T(8,128)S(1)} %cholesky.771), custom_call_target="Cholesky" | custom-call | tf_op jit(solution)/shard_map/jit(cholesky)/cholesky | solution.py:49
  502.6 10.0 %custom-call.71 = f32[1,1,128,128]{2,3,1,0:T(8,128)S(1)} custom-call(f32[1,1,128,128]{3,2,1,0:T(8,128)S(1)} %get-tuple-element.64), custom_call_target="InvertDiagBlocksLowerTriangular" | custom-call | tf_op jit(solution)/shard_map/jit(cholesky)/cholesky | solution.py:49
  514.2 11.7 %custom-call.72 = f32[1,128,128]{2,1,0:T(8,128)S(1)} custom-call(f32[1,128,128]{2,1,0:T(8,128)S(1)} %cholesky.776), custom_call_target="Cholesky" | custom-call | tf_op jit(solution)/shard_map/jit(cholesky)/cholesky | solution.py:49
  526.7 9.8 %custom-call.73 = f32[1,1,128,128]{2,3,1,0:T(8,128)S(1)} custom-call(f32[1,1,128,128]{3,2,1,0:T(8,128)S(1)} %get-tuple-element.61), custom_call_target="InvertDiagBlocksLowerTriangular" | custom-call | tf_op jit(solution)/shard_map/jit(cholesky)/cholesky | solution.py:49
  537.9 11.7 %custom-call.74 = f32[1,128,128]{2,1,0:T(8,128)S(1)} custom-call(f32[1,128,128]{2,1,0:T(8,128)S(1)} %fusion.18), custom_call_target="Cholesky" | custom-call | tf_op jit(solution)/shard_map/jit(cholesky)/cholesky | solution.py:49
  554.6 2.9 fusion.36
  557.5 2.6 copy.20
  560.1 1.5 fusion.34
  562.6 11.7 %custom-call.75 = f32[1,128,128]{2,1,0:T(8,128)S(1)} custom-call(f32[1,128,128]{2,1,0:T(8,128)S(1)} %cholesky.780), custom_call_target="Cholesky" | custom-call | tf_op jit(solution)/shard_map/jit(cholesky)/cholesky | solution.py:57
  575.0 9.8 %custom-call.76 = f32[1,1,128,128]{2,3,1,0:T(8,128)S(1)} custom-call(f32[1,1,128,128]{3,2,1,0:T(8,128)S(1)} %get-tuple-element.57), custom_call_target="InvertDiagBlocksLowerTriangular" | custom-call | tf_op jit(solution)/shard_map/jit(cholesky)/cholesky | solution.py:57
  587.5 11.9 %custom-call.77 = f32[1,128,128]{2,1,0:T(8,128)S(1)} custom-call(f32[1,128,128]{2,1,0:T(8,128)S(1)} %cholesky.784), custom_call_target="Cholesky" | custom-call | tf_op jit(solution)/shard_map/jit(cholesky)/cholesky | solution.py:57
  600.0 9.8 %custom-call.78 = f32[1,1,128,128]{2,3,1,0:T(8,128)S(1)} custom-call(f32[1,1,128,128]{3,2,1,0:T(8,128)S(1)} %get-tuple-element.54), custom_call_target="InvertDiagBlocksLowerTriangular" | custom-call | tf_op jit(solution)/shard_map/jit(cholesky)/cholesky | solution.py:57
  611.4 11.7 %custom-call.79 = f32[1,128,128]{2,1,0:T(8,128)S(1)} custom-call(f32[1,128,128]{2,1,0:T(8,128)S(1)} %cholesky.789), custom_call_target="Cholesky" | custom-call | tf_op jit(solution)/shard_map/jit(cholesky)/cholesky | solution.py:57
  623.8 9.8 %custom-call.80 = f32[1,1,128,128]{2,3,1,0:T(8,128)S(1)} custom-call(f32[1,1,128,128]{3,2,1,0:T(8,128)S(1)} %get-tuple-element.51), custom_call_target="InvertDiagBlocksLowerTriangular" | custom-call | tf_op jit(solution)/shard_map/jit(cholesky)/cholesky | solution.py:57
  635.1 11.9 %custom-call.81 = f32[1,128,128]{2,1,0:T(8,128)S(1)} custom-call(f32[1,128,128]{2,1,0:T(8,128)S(1)} %fusion.19), custom_call_target="Cholesky" | custom-call | tf_op jit(solution)/shard_map/jit(cholesky)/cholesky | solution.py:57
  652.1 13.9 %while.5 = (s32[]{:T(128)}, f32[512,512]{1,0:T(8,128)}, s32[4,2]{0,1:T(2,128)S(1)}, f32[4,128,128]{2,1,0:T(8,128)}, s32[]{:T(128)}) while((s32[]{:T(128)}, f32[512,512]{1,0:T(8,128)}, s32[4,2]{0,1:T(2,128)S(1)}, f32[4,128,128]{2,1,0:T(8,128)}, s32[]{:T(128)}) %tuple.85), condition=%wide.while_cond.clone, body=%wide.while_body.clone.sunk | while | flops 2 | bytes 132205 | solution.py:32
  652.7 2.9 bitcast_dynamic-update-slice_fusion.5
  656.2 2.9 bitcast_dynamic-update-slice_fusion.5
  659.7 2.9 bitcast_dynamic-update-slice_fusion.5
  663.2 2.8 bitcast_dynamic-update-slice_fusion.5
  666.0 40.2 %custom-call.82 = f32[4,128,128]{1,2,0:T(8,128)S(1)} custom-call(f32[4,128,128]{2,1,0:T(8,128)} %get-tuple-element.19), custom_call_target="InvertDiagBlocksLowerTriangular" | custom-call | tf_op jit(solution)/shard_map/jit(_solve_triangular)/triangular_solve | solution.py:32
  707.6 1.6 convolution_subtract_fusion.1
  709.6 1.9 convolution_subtract_fusion
  711.9 2.4 convolution_subtract_fusion.4
  715.9 4.5 gather_fusion.1
  720.4 3.4 collective-permute-start.2
  727.2 5.8 psum.23
  (153 shorter events, 65.2 us)
Async XLA Ops:
  7.2 1.0 copy-start
  7.2 100.4 %all-reduce.4.cloned.1.call-start = ((), (), s32[]{:S(2)}) async-start(), calls=%async_computation | async-start | bytes 2097152 | tf_op jit(solution)/shard_map/psum | solution.py:44
  10.3 452.2 %all-reduce.6.cloned.1.call-start = ((), (), s32[]{:S(2)}) async-start(), calls=%async_computation.1 | async-start | bytes 2097152 | tf_op jit(solution)/shard_map/psum | solution.py:75
  107.6 1.7 copy-start.1
  109.5 1.0 copy-start.10
  201.8 2.6 copy-start.3
  205.9 1.0 copy-start.7
  307.5 42.7 %copy-start.6 = (f32[1,512,512]{1,2,0:T(8,128)S(1)}, f32[1,512,512]{1,2,0:T(8,128)}, u32[]{:S(2)}) copy-start(f32[1,512,512]{1,2,0:T(8,128)} %fusion.43) | copy-start | bytes 3145732
  356.5 8.3 %collective-permute-start = (f32[256,256]{0,1:T(8,128)S(1)}, f32[256,256]{0,1:T(8,128)S(1)}, u32[]{:S(2)}, u32[]{:S(2)}) collective-permute-start(f32[256,256]{0,1:T(8,128)S(1)} %fusion.76), channel_id=1, source_target_pairs={{0,1},{2,3},{4,5},{6,7},{8,9},{10,11},{12,13},{14,15},{16,17},{18,... | collective-permute-start | bytes 786440 | tf_op jit(solution)/shard_map/ppermute | solution.py:12
  359.9 9.0 %collective-permute-start.1 = (f32[256,256]{0,1:T(8,128)S(1)}, f32[256,256]{0,1:T(8,128)S(1)}, u32[]{:S(2)}, u32[]{:S(2)}) collective-permute-start(f32[256,256]{0,1:T(8,128)S(1)} %slice_bitcast_fusion.11), channel_id=1, source_target_pairs={{1,0},{3,2},{5,4},{7,6},{9,8},{11,10},{13,12},{15,14},{17,16},{19,... | collective-permute-start | bytes 786440 | tf_op jit(solution)/shard_map/ppermute | solution.py:12
  462.5 1.7 copy-start.2
  464.4 1.0 copy-start.9
  557.5 2.6 copy-start.4
  561.6 1.0 copy-start.8
  666.0 43.6 %copy-start.5 = (f32[1,512,512]{1,2,0:T(8,128)S(1)}, f32[1,512,512]{1,2,0:T(8,128)}, u32[]{:S(2)}) copy-start(f32[1,512,512]{1,2,0:T(8,128)} %fusion.45) | copy-start | bytes 3145732
  720.4 13.1 %collective-permute-start.2 = (f32[256,256]{0,1:T(8,128)S(1)}, f32[256,256]{0,1:T(8,128)S(1)}, u32[]{:S(2)}, u32[]{:S(2)}) collective-permute-start(f32[256,256]{0,1:T(8,128)S(1)} %fusion.79), channel_id=1, source_target_pairs={{0,1},{2,3},{4,5},{6,7},{8,9},{10,11},{12,13},{14,15},{16,17},{18,... | collective-permute-start | bytes 786440 | tf_op jit(solution)/shard_map/ppermute | solution.py:12
  723.8 9.7 %collective-permute-start.3 = (f32[256,256]{0,1:T(8,128)S(1)}, f32[256,256]{0,1:T(8,128)S(1)}, u32[]{:S(2)}, u32[]{:S(2)}) collective-permute-start(f32[256,256]{0,1:T(8,128)S(1)} %slice_bitcast_fusion), channel_id=1, source_target_pairs={{1,0},{3,2},{5,4},{7,6},{9,8},{11,10},{13,12},{15,14},{17,16},{19,... | collective-permute-start | bytes 786440 | tf_op jit(solution)/shard_map/ppermute | solution.py:12
Sparse Core Ops, SparseCore 0:
  11.5 96.0 all-reduce.3
  371.3 91.1 all-reduce.5
where the time goes:
time: 753 us; the launch traced here: 742 us
  other arithmetic  409 us (54%)
  waiting for transfers between devices  191 us (25%)
  matrix products  50.8 us (7%)
  local copies, waits for them, and re-layouts  50.6 us (7%)
  between operations  25.6 us (3%)
  starting transfers between devices  9.45 us (1%)
    psum x2, waiting for transfers between devices, body(): pair_gram = lax.psum(pair_grams(pair_blocks), 'row')  183 us
    another operation x30, other arithmetic, body(): second = jnp.linalg.cholesky(inner_gram)  159 us
    another operation x29, other arithmetic, body(): lower_factor = jnp.linalg.cholesky(pair_gram)  159 us
    another operation x5, other arithmetic, lower_solve(): return jax.scipy.linalg.solve_triangular(second, right_side, lower=True)  81.9 us
    another operation x27, local copies, waits for them, and re-layouts, lower_solve(): return jax.scipy.linalg.solve_triangular(second, right_side, lower=True)  26.1 us
    another operation x14, matrix products, lower_solve(): return jax.scipy.linalg.solve_triangular(second, right_side, lower=True)  17 us
  transfers between devices with their start and end apart: 6, of which 4 were waited for; matrix products, arithmetic and copies ran while one was open for 1% of the time, Pallas kernels for 0%

commit v1 on v0

--- a/solution.py
+++ b/solution.py
@@ -1,6 +1,8 @@
 import jax
 import jax.numpy as jnp
 from jax import lax
+from jax.experimental import pallas as pl
+from jax.experimental.pallas import tpu as pltpu
 from jax.sharding import PartitionSpec as P
 
 STEPS = 2
@@ -22,14 +24,141 @@
     )
 
 
-def coupling_term(pair_gram, width):
-    diagonal = jnp.diagonal(pair_gram, axis1=1, axis2=2)
-    cross = pair_gram[:, :width, width:]
-    return jnp.sum(cross * cross / (diagonal[:, :width, None] * diagonal[:, None, width:]))
-
-
-def lower_solve(second, right_side):
-    return jax.scipy.linalg.solve_triangular(second, right_side, lower=True)
+LEAF = 128
+GROUP = 8
+AHEAD = 4
+
+
+def mat(left, right, contract):
+    return lax.dot_general(
+        left,
+        right,
+        (contract, ((), ())),
+        precision=lax.Precision.HIGHEST,
+        preferred_element_type=jnp.float32,
+    )
+
+
+def spread(row, shape):
+    return jnp.broadcast_to(row, shape)
+
+
+def inverse_factors(blocks):
+    shape = (GROUP, LEAF)
+    groups = LEAF // GROUP
+    lane = lax.broadcasted_iota(jnp.int32, shape, 1)
+    sub = lax.broadcasted_iota(jnp.int32, shape, 0)
+    works = [[block[GROUP * i : GROUP * (i + 1), :] for i in range(groups)] for block in blocks]
+    for start in range(0, LEAF, AHEAD):
+        first = start // GROUP
+        columns = [
+            [
+                [spread(work[i][:, start + t : start + t + 1], shape) for i in range(first, groups)]
+                for t in range(AHEAD)
+            ]
+            for work in works
+        ]
+        for t in range(AHEAD):
+            pivot = start + t
+            inside = pivot % GROUP
+            for work, column in zip(works, columns):
+                own = column[t]
+                scale = 1.0 / spread(own[0][inside : inside + 1, :], shape)
+                for later in range(t + 1, AHEAD):
+                    place = inside + later - t
+                    factor = spread(own[0][place : place + 1, :], shape) * scale
+                    column[later] = [c - o * factor for c, o in zip(column[later], own)]
+                row = spread(work[first][inside : inside + 1, :], shape)
+                here = lane == pivot
+                row = jnp.where(here, 1.0, row) * scale
+                for i in range(first, groups):
+                    held = work[i]
+                    if i == first:
+                        below = sub > inside
+                        updated = jnp.where(here, 0.0, held) - own[0] * row
+                        work[i] = jnp.where(below, updated, held)
+                    else:
+                        work[i] = jnp.where(here, 0.0, held) - own[i - first] * row
+    results = []
+    for work in works:
+        full = jnp.concatenate(work, axis=0)
+        rows = lax.broadcasted_iota(jnp.int32, full.shape, 0)
+        lanes = lax.broadcasted_iota(jnp.int32, full.shape, 1)
+        pivots = jnp.sum(jnp.where(rows == lanes, full, 0.0), axis=1, keepdims=True)
+        unit = jnp.where(rows == lanes, 1.0, jnp.where(rows > lanes, full, 0.0))
+        results.append(unit * lax.rsqrt(pivots))
+    return results
+
+
+def rotation_kernel(gram_ref, turn_ref, term_ref, work, part, inner):
+    size = gram_ref.shape[0]
+    half = size // 2
+    count = size // LEAF
+    gram = gram_ref[...]
+    rows = lax.broadcasted_iota(jnp.int32, (size, size), 0)
+    lanes = lax.broadcasted_iota(jnp.int32, (size, size), 1)
+    diagonal = jnp.where(rows == lanes, gram, 0.0)
+    down = jnp.sum(diagonal, axis=1, keepdims=True)[:half]
+    across = jnp.sum(diagonal, axis=0, keepdims=True)[:, half:]
+    cross = gram[:half, half:]
+    total = jnp.sum(cross * cross / (down * across), axis=1, keepdims=True)
+    total = jnp.sum(total, axis=0, keepdims=True)
+    term_ref[...] = jnp.broadcast_to(total, term_ref.shape)
+
+    eye = (
+        lax.broadcasted_iota(jnp.int32, (LEAF, LEAF), 0)
+        == lax.broadcasted_iota(jnp.int32, (LEAF, LEAF), 1)
+    ).astype(jnp.float32)
+    work[...] = gram
+    turn_ref[...] = jnp.zeros_like(turn_ref)
+    inner[...] = eye
+    place_lanes = lax.broadcasted_iota(jnp.int32, (LEAF, size), 1)
+
+    def stage(index, carry):
+        now = jnp.minimum(index, count - 1)
+        here = pl.ds(pl.multiple_of(now * LEAF, LEAF), LEAF)
+        outer_inverse, inner_inverse = inverse_factors([work[here, here], inner[...]])
+
+        @pl.when(index > 0)
+        def _():
+            before = pl.ds(pl.multiple_of((index - 1) * LEAF, LEAF), LEAF)
+            turn_ref[before, :] = mat(inner_inverse, part[...], ((1,), (0,)))
+
+        @pl.when(index < count)
+        def _():
+            factor = mat(outer_inverse, work[here, :], ((1,), (0,)))
+            factor = jnp.where(place_lanes >= now * LEAF, factor, 0.0)
+            turned = turn_ref[...]
+            overlap = mat(factor, turned, ((1,), (1,)))
+            rest = factor - mat(overlap, turned, ((1,), (0,)))
+            part[...] = rest
+            inner[...] = mat(rest, rest, ((1,), (1,)))
+            work[...] -= mat(factor, factor, ((0,), (0,)))
+
+        return carry
+
+    lax.fori_loop(0, count + 1, stage, 0)
+
+
+def rotation_of(pair_gram):
+    size = pair_gram.shape[0]
+    vmem = pl.BlockSpec(memory_space=pltpu.VMEM)
+    turn, term = pl.pallas_call(
+        rotation_kernel,
+        out_shape=(
+            jax.ShapeDtypeStruct((size, size), jnp.float32),
+            jax.ShapeDtypeStruct((8, 128), jnp.float32),
+        ),
+        in_specs=[vmem],
+        out_specs=(vmem, vmem),
+        scratch_shapes=[
+            pltpu.VMEM((size, size), jnp.float32),
+            pltpu.VMEM((LEAF, size), jnp.float32),
+            pltpu.VMEM((LEAF, LEAF), jnp.float32),
+        ],
+        compiler_params=pltpu.CompilerParams(vmem_limit_bytes=32 << 20),
+    )(pair_gram)
+    return turn, term[0, 0]
 
 
 def body(matrix):
@@ -44,22 +173,12 @@
     pair_gram = lax.psum(pair_grams(pair_blocks), "row")
     coupling_terms = []
     for step_index in range(STEPS):
-        local_term = coupling_term(pair_gram, width)
+        turn, local_term = rotation_of(pair_gram[0])
         coupling_terms.append(local_term)
-        lower_factor = jnp.linalg.cholesky(pair_gram)
-        inner_gram = jnp.einsum(
-            "pik,pil->pkl",
-            lower_factor,
-            lower_factor,
-            precision=lax.Precision.HIGHEST,
-            preferred_element_type=jnp.float32,
-        )
-        second = jnp.linalg.cholesky(inner_gram)
-        rotation = jnp.swapaxes(lower_solve(second, jnp.swapaxes(lower_factor, 1, 2)), 1, 2)
         turned = jnp.einsum(
-            "prk,pkl->prl",
+            "prk,lk->prl",
             pair_blocks,
-            rotation,
+            turn,
             precision=lax.Precision.HIGHEST,
             preferred_element_type=jnp.float32,
         )

time: 753 us -> 337 us (0.45); the launches traced: 742 us -> 337 us
  other arithmetic: 409 us -> 2.1 us
  Pallas kernels: 0 us -> 97.5 us
  local copies, waits for them, and re-layouts: 50.6 us -> 5.5 us
  matrix products: 50.8 us -> 6.17 us
  between operations: 25.6 us -> 14.2 us
    another operation x64 -> x0, other arithmetic: 399 us -> none  [the longest x30 159 us: body(): second = jnp.linalg.cholesky(inner_gram)]
    pallas_call x0 -> x2, Pallas kernels: none -> 97.5 us  [rotation_of(): pl.pallas_call(rotation_kernel, out_shape=(jax.ShapeDtypeStruct((size, si...]
    another operation x38 -> x0, matrix products: 38.8 us -> none  [the longest x14 17 us: lower_solve(): return jax.scipy.linalg.solve_triangular(second, right_side, lower=True)]
    another operation x43 -> x0, local copies, waits for them, and re-layouts: 26.7 us -> none  [the longest x27 26.1 us: lower_solve(): return jax.scipy.linalg.solve_triangular(second, right_side, lower=True)]
    gather x2 -> x0, local copies, waits for them, and re-layouts: 9.27 us -> none  [coupling_term(): diagonal = jnp.diagonal(pair_gram, axis1=1, axis2=2)]
where the time goes in v1:
time: 337 us
  waiting for transfers between devices  195 us (58%)
  Pallas kernels  97.5 us (29%)
  between operations  14.2 us (4%)
  starting transfers between devices  9.62 us (3%)
  blocking collectives  6.47 us (2%)
  matrix products  6.17 us (2%)
  local copies, waits for them, and re-layouts  5.5 us (2%)
    psum x2, waiting for transfers between devices, body(): pair_gram = lax.psum(pair_grams(pair_blocks), 'row')  188 us
    pallas_call x2, Pallas kernels, rotation_of(): pl.pallas_call(rotation_kernel, out_shape=(jax.ShapeDtypeStruct((size, si...  97.5 us
    ppermute x4, starting transfers between devices, from_behind(): lax.ppermute(value, axis, [(source, source + steps) for source in range(f...  9.54 us
    ppermute x4, waiting for transfers between devices, from_behind(): lax.ppermute(value, axis, [(source, source + steps) for source in range(f...  7.56 us
  transfers between devices with their start and end apart: 6, of which 4 were waited for; matrix products, arithmetic and copies ran while one was open for 1% of the time, Pallas kernels for 0%

profile of v1, /device:TPU:0, one launch (start us, length us, event | category | flops | bytes accessed | tf_op | source)
XLA Modules:
  0.0 336.9 jit_solution(3336766219487323583)
XLA Ops:
  7.2 0.0 copy-start
  7.2 0.0 all-reduce.3.cloned.1.call-start
  7.2 1.0 copy-done
  8.2 2.1 fusion.9
  10.3 0.0 all-reduce.3.cloned.1.call-update
  10.3 0.0 all-reduce.5.cloned.1.call-start
  10.4 97.0 %all-reduce.3.cloned.1.call-done.gram_ref = f32[512,512]{1,0:T(8,128)} async-done(((f32[512,512]{1,0:T(8,128)}), f32[512,512]{1,0:T(8,128)}) %all-reduce.3.cloned.1.call-update) | async-done | bytes 1048592 | tf_op jit(solution)/shard_map/psum | solution.py:173
  107.3 0.0 copy-start.1
  107.3 1.2 copy-done.1
  108.5 48.8 %shard_map.30 = (f32[512,512]{1,0:T(8,128)S(1)}, f32[8,128]{1,0:T(8,128)S(1)}) custom-call(f32[512,512]{1,0:T(8,128)S(1)} %copy-done.1), custom_call_target="tpu_custom_call" | custom-call | tf_op jit(solution)/shard_map/pallas_call | solution.py:146
  157.3 1.0 convolution_bitcast_fusion.1
  158.4 3.4 %collective-permute-start = (f32[256,256]{0,1:T(8,128)S(1)}, f32[256,256]{0,1:T(8,128)S(1)}, u32[]{:S(2)}, u32[]{:S(2)}) collective-permute-start(f32[256,256]{0,1:T(8,128)S(1)} %fusion.3), channel_id=1, source_target_pairs={{0,1},{2,3},{4,5},{6,7},{8,9},{10,11},{12,13},{14,15},{16,17},{18,... | collective-permute-start | bytes 786440 | tf_op jit(solution)/shard_map/ppermute | solution.py:14
  161.8 1.5 collective-permute-start.1
  163.3 3.4 %collective-permute-done = f32[256,256]{0,1:T(8,128)S(1)} collective-permute-done((f32[256,256]{0,1:T(8,128)S(1)}, f32[256,256]{0,1:T(8,128)S(1)}, u32[]{:S(2)}, u32[]{:S(2)}) %collective-permute-start) | collective-permute-done | bytes 262176 | tf_op jit(solution)/shard_map/ppermute | solution.py:14
  166.7 4.1 %collective-permute-done.1 = f32[256,256]{0,1:T(8,128)S(1)} collective-permute-done((f32[256,256]{0,1:T(8,128)S(1)}, f32[256,256]{0,1:T(8,128)S(1)}, u32[]{:S(2)}, u32[]{:S(2)}) %collective-permute-start.1) | collective-permute-done | bytes 262176 | tf_op jit(solution)/shard_map/ppermute | solution.py:14
  170.9 0.1 fusion.2
  170.9 2.1 fusion
  173.0 0.0 all-reduce.5.cloned.1.call-update
  173.0 0.5 slice.22
  173.5 90.8 %all-reduce.5.cloned.1.call-done.gram_ref = f32[512,512]{1,0:T(8,128)} async-done(((f32[512,512]{1,0:T(8,128)}), f32[512,512]{1,0:T(8,128)}) %all-reduce.5.cloned.1.call-update) | async-done | bytes 1048592 | tf_op jit(solution)/shard_map/psum | solution.py:194
  264.3 0.0 copy-start.2
  264.3 1.2 copy-done.2
  265.5 48.8 %shard_map.31 = (f32[512,512]{1,0:T(8,128)S(1)}, f32[8,128]{1,0:T(8,128)S(1)}) custom-call(f32[512,512]{1,0:T(8,128)S(1)} %copy-done.2), custom_call_target="tpu_custom_call" | custom-call | tf_op jit(solution)/shard_map/pallas_call | solution.py:146
  314.3 1.0 convolution_bitcast_fusion
  315.4 0.5 slice.23
  315.9 3.4 %collective-permute-start.2 = (f32[256,256]{0,1:T(8,128)S(1)}, f32[256,256]{0,1:T(8,128)S(1)}, u32[]{:S(2)}, u32[]{:S(2)}) collective-permute-start(f32[256,256]{0,1:T(8,128)S(1)} %fusion.6), channel_id=1, source_target_pairs={{0,1},{2,3},{4,5},{6,7},{8,9},{10,11},{12,13},{14,15},{16,17},{18,... | collective-permute-start | bytes 786440 | tf_op jit(solution)/shard_map/ppermute | solution.py:14
  319.3 1.3 collective-permute-start.3
  320.6 1.4 pad_maximum_fusion.4
  322.0 6.5 %psum.23 = f32[2]{0:T(128)S(1)} all-reduce(f32[2]{0:T(128)S(1)} %pad_maximum_fusion.4), channel_id=1, replica_groups=mesh['row'=16,'col'=2] {'col'}, use_global_device_ids=true, to_apply=%region_2.3 | all-reduce | flops 2 | bytes 16 | tf_op jit(solution)/shard_map/psum | solution.py:195
  328.4 0.5 multiply_sqrt_fusion
  329.0 0.0 collective-permute-done.2
  329.0 0.0 collective-permute-done.3
  329.0 0.1 fusion.5
  329.1 1.0 copy.4
  (5 shorter events, 0.1 us)
Async XLA Ops:
  7.2 1.0 copy-start
  7.2 100.1 %all-reduce.3.cloned.1.call-start = ((), (), s32[]{:S(2)}) async-start(), calls=%async_computation | async-start | bytes 2097152 | tf_op jit(solution)/shard_map/psum | solution.py:173
  10.3 254.0 %all-reduce.5.cloned.1.call-start = ((), (), s32[]{:S(2)}) async-start(), calls=%async_computation.1 | async-start | bytes 2097152 | tf_op jit(solution)/shard_map/psum | solution.py:194
  107.3 1.2 copy-start.1
  158.4 8.3 %collective-permute-start = (f32[256,256]{0,1:T(8,128)S(1)}, f32[256,256]{0,1:T(8,128)S(1)}, u32[]{:S(2)}, u32[]{:S(2)}) collective-permute-start(f32[256,256]{0,1:T(8,128)S(1)} %fusion.3), channel_id=1, source_target_pairs={{0,1},{2,3},{4,5},{6,7},{8,9},{10,11},{12,13},{14,15},{16,17},{18,... | collective-permute-start | bytes 786440 | tf_op jit(solution)/shard_map/ppermute | solution.py:14
  161.8 9.0 %collective-permute-start.1 = (f32[256,256]{0,1:T(8,128)S(1)}, f32[256,256]{0,1:T(8,128)S(1)}, u32[]{:S(2)}, u32[]{:S(2)}) collective-permute-start(f32[256,256]{0,1:T(8,128)S(1)} %slice_bitcast_fusion.2), channel_id=1, source_target_pairs={{1,0},{3,2},{5,4},{7,6},{9,8},{11,10},{13,12},{15,14},{17,16},{19,... | collective-permute-start | bytes 786440 | tf_op jit(solution)/shard_map/ppermute | solution.py:14
  264.3 1.2 copy-start.2
  315.9 13.1 %collective-permute-start.2 = (f32[256,256]{0,1:T(8,128)S(1)}, f32[256,256]{0,1:T(8,128)S(1)}, u32[]{:S(2)}, u32[]{:S(2)}) collective-permute-start(f32[256,256]{0,1:T(8,128)S(1)} %fusion.6), channel_id=1, source_target_pairs={{0,1},{2,3},{4,5},{6,7},{8,9},{10,11},{12,13},{14,15},{16,17},{18,... | collective-permute-start | bytes 786440 | tf_op jit(solution)/shard_map/ppermute | solution.py:14
  319.3 9.7 %collective-permute-start.3 = (f32[256,256]{0,1:T(8,128)S(1)}, f32[256,256]{0,1:T(8,128)S(1)}, u32[]{:S(2)}, u32[]{:S(2)}) collective-permute-start(f32[256,256]{0,1:T(8,128)S(1)} %slice_bitcast_fusion), channel_id=1, source_target_pairs={{1,0},{3,2},{5,4},{7,6},{9,8},{11,10},{13,12},{15,14},{17,16},{19,... | collective-permute-start | bytes 786440 | tf_op jit(solution)/shard_map/ppermute | solution.py:14
Sparse Core Ops, SparseCore 0:
  11.5 95.7 all-reduce.2
  173.1 91.1 all-reduce.4

commit v2 on v1

--- a/solution.py
+++ b/solution.py
@@ -1,3 +1,5 @@
+import functools
+
 import jax
 import jax.numpy as jnp
 from jax import lax
@@ -12,16 +14,6 @@
     count = lax.axis_size(axis)
     first, last = (max(0, -steps), min(count, count - steps))
     return lax.ppermute(value, axis, [(source, source + steps) for source in range(first, last)])
-
-
-def pair_grams(pair_blocks):
-    return jnp.einsum(
-        "prk,prl->pkl",
-        pair_blocks,
-        pair_blocks,
-        precision=lax.Precision.HIGHEST,
-        preferred_element_type=jnp.float32,
-    )
 
 
 LEAF = 128
@@ -91,16 +83,15 @@
 
 
 def rotation_kernel(gram_ref, turn_ref, term_ref, work, part, inner):
-    size = gram_ref.shape[0]
-    half = size // 2
+    half = gram_ref.shape[1]
+    size = 2 * half
     count = size // LEAF
-    gram = gram_ref[...]
-    rows = lax.broadcasted_iota(jnp.int32, (size, size), 0)
-    lanes = lax.broadcasted_iota(jnp.int32, (size, size), 1)
-    diagonal = jnp.where(rows == lanes, gram, 0.0)
-    down = jnp.sum(diagonal, axis=1, keepdims=True)[:half]
-    across = jnp.sum(diagonal, axis=0, keepdims=True)[:, half:]
-    cross = gram[:half, half:]
+    same = lax.broadcasted_iota(jnp.int32, (half, half), 0) == lax.broadcasted_iota(
+        jnp.int32, (half, half), 1
+    )
+    top, cross, bottom = (gram_ref[half * i : half * (i + 1), :] for i in range(3))
+    down = jnp.sum(jnp.where(same, top, 0.0), axis=1, keepdims=True)
+    across = jnp.sum(jnp.where(same, bottom, 0.0), axis=0, keepdims=True)
     total = jnp.sum(cross * cross / (down * across), axis=1, keepdims=True)
     total = jnp.sum(total, axis=0, keepdims=True)
     term_ref[...] = jnp.broadcast_to(total, term_ref.shape)
@@ -109,7 +100,10 @@
         lax.broadcasted_iota(jnp.int32, (LEAF, LEAF), 0)
         == lax.broadcasted_iota(jnp.int32, (LEAF, LEAF), 1)
     ).astype(jnp.float32)
-    work[...] = gram
+    work[:half, :half] = top
+    work[:half, half:] = cross
+    work[half:, :half] = jnp.zeros_like(cross)
+    work[half:, half:] = bottom
     turn_ref[...] = jnp.zeros_like(turn_ref)
     inner[...] = eye
     place_lanes = lax.broadcasted_iota(jnp.int32, (LEAF, size), 1)
@@ -141,7 +135,7 @@
 
 
 def rotation_of(pair_gram):
-    size = pair_gram.shape[0]
+    size = 2 * pair_gram.shape[1]
     vmem = pl.BlockSpec(memory_space=pltpu.VMEM)
     turn, term = pl.pallas_call(
         rotation_kernel,
@@ -161,6 +155,104 @@
     return turn, term[0, 0]
 
 
+def reduce_kernel(count, pair_ref, out_ref, mine, half_in, half, part_in, part, chunk_in, send, recv):
+    width = pair_ref.shape[1] // 2
+    rows = out_ref.shape[0]
+    planes = count // 4
+    place = lax.axis_index("row")
+    core = lax.rem(place, 2)
+    side = lax.rem(place // 2, 2)
+    plane = place // 4
+    other_core = place + 1 - 2 * core
+    other_side = place + 2 - 4 * side
+    others = [4 * lax.rem(plane + step, planes) + 2 * side + core for step in range(1, planes)]
+
+    barrier = pltpu.get_barrier_semaphore()
+    for peer in [other_core, other_side] + others:
+        pl.semaphore_signal(
+            barrier, inc=1, device_id={"row": peer}, device_id_type=pl.DeviceIdType.MESH
+        )
+
+    top = pair_ref[:, :width]
+    bottom = pair_ref[:, width:]
+    mine[:width, :] = mat(top, top, ((0,), (0,)))
+    mine[width : 2 * width, :] = mat(top, bottom, ((0,), (0,)))
+    mine[2 * width :, :] = mat(bottom, bottom, ((0,), (0,)))
+    pl.semaphore_wait(barrier, 1 + planes)
+
+    def put(source, target, index, peer):
+        copy = pltpu.make_async_remote_copy(
+            src_ref=source,
+            dst_ref=target,
+            send_sem=send.at[index],
+            recv_sem=recv.at[index],
+            device_id={"row": peer},
+            device_id_type=pl.DeviceIdType.MESH,
+        )
+        copy.start()
+        return copy
+
+    def span(start, length):
+        return pl.ds(pl.multiple_of(start, 8), length)
+
+    large, middle, small = rows // 2, rows // 4, rows // count
+    put(mine.at[span((1 - core) * large, large)], half_in, 0, other_core).wait()
+    half[...] = mine[span(core * large, large), :] + half_in[...]
+    put(half.at[span((1 - side) * middle, middle)], part_in, 1, other_side).wait()
+    part[...] = half[span(side * middle, middle), :] + part_in[...]
+    copies = []
+    for step in range(1, planes):
+        there = lax.rem(plane + step, planes)
+        source = part.at[span(there * small, small)]
+        copies.append(put(source, chunk_in.at[step - 1], 1 + step, others[step - 1]))
+    total = part[span(plane * small, small), :]
+    for step in range(1, planes):
+        copies[step - 1].wait()
+        total += chunk_in[step - 1]
+
+    base = core * large + side * middle
+    own = span(base + plane * small, small)
+    out_ref[own, :] = total
+    shift = 1 + planes
+    copies = [
+        put(out_ref.at[own], out_ref.at[own], shift + 1 + step, others[step - 1])
+        for step in range(1, planes)
+    ]
+    for copy in copies:
+        copy.wait()
+    quarter = span(base, middle)
+    put(out_ref.at[quarter], out_ref.at[quarter], shift + 1, other_side).wait()
+    whole = span(core * large, large)
+    put(out_ref.at[whole], out_ref.at[whole], shift, other_core).wait()
+
+
+def reduced_gram(pair):
+    width = pair.shape[1] // 2
+    rows = 3 * width
+    count = lax.axis_size("row")
+    planes = count // 4
+    vmem = pl.BlockSpec(memory_space=pltpu.VMEM)
+    return pl.pallas_call(
+        functools.partial(reduce_kernel, count),
+        out_shape=jax.ShapeDtypeStruct((rows, width), jnp.float32),
+        in_specs=[vmem],
+        out_specs=vmem,
+        scratch_shapes=[
+            pltpu.VMEM((rows, width), jnp.float32),
+            pltpu.VMEM((rows // 2, width), jnp.float32),
+            pltpu.VMEM((rows // 2, width), jnp.float32),
+            pltpu.VMEM((rows // 4, width), jnp.float32),
+            pltpu.VMEM((rows // 4, width), jnp.float32),
+            pltpu.VMEM((planes - 1, rows // count, width), jnp.float32),
+            pltpu.SemaphoreType.DMA((2 + 2 * planes,)),
+            pltpu.SemaphoreType.DMA((2 + 2 * planes,)),
+        ],
+        compiler_params=pltpu.CompilerParams(
+            collective_id=0, has_side_effects=True, vmem_limit_bytes=32 << 20
+        ),
+    )(pair)
+
+
 def body(matrix):
     width = matrix.shape[1] // 2
     col_place = lax.axis_index("col")
@@ -170,10 +262,10 @@
     top_block = matrix[:, :width]
     bottom_block = matrix[:, width:]
     pair_blocks = matrix[None]
-    pair_gram = lax.psum(pair_grams(pair_blocks), "row")
+    pair_gram = reduced_gram(pair_blocks[0])
     coupling_terms = []
     for step_index in range(STEPS):
-        turn, local_term = rotation_of(pair_gram[0])
+        turn, local_term = rotation_of(pair_gram)
         coupling_terms.append(local_term)
         turned = jnp.einsum(
             "prk,lk->prl",
@@ -191,7 +283,7 @@
         bottom_block = jnp.where(last_col, new_top, arrived_bottom)
         pair_blocks = jnp.concatenate([top_block, bottom_block], axis=1)[None]
         if step_index + 1 < STEPS:
-            pair_gram = lax.psum(pair_grams(pair_blocks), "row")
+            pair_gram = reduced_gram(pair_blocks[0])
     totals = lax.psum(jnp.stack(coupling_terms), "col")
     coupling = jnp.sqrt(totals / (1.0 * lax.axis_size("col") * width))
     rotated = jnp.concatenate([top_block, bottom_block], axis=1)

time: 337 us -> 186 us (0.55)
  waiting for transfers between devices: 195 us -> 8.2 us
  Pallas kernels: 97.5 us -> 155 us
  between operations: 14.2 us -> 0.78 us
  matrix products: 6.17 us -> 2.11 us
  local copies, waits for them, and re-layouts: 5.5 us -> 2.1 us
    psum x2 -> x0, waiting for transfers between devices: 188 us -> none  [body(): pair_gram = lax.psum(pair_grams(pair_blocks), 'row')]
    pallas_call x0 -> x2, Pallas kernels: none -> 57.1 us  [reduced_gram(): pl.pallas_call(functools.partial(reduce_kernel, count), out_shape=jax.Sha...]
    dot_general x2 -> x0, matrix products: 4.14 us -> none  [pair_grams(): jnp.einsum('prk,prl->pkl', pair_blocks, pair_blocks, precision=lax.Precis...]
    unnamed x7 -> x2, local copies, waits for them, and re-layouts: 4.44 us -> 1.03 us
  transfers between devices with their start and end apart: 6 -> 4, of which waited for: 4 -> 2; matrix products, arithmetic and copies ran while one was open for 1% -> 1% of each run, Pallas kernels for 0% -> 0%
where the time goes in v2:
time: 186 us
  Pallas kernels  155 us (83%)
  waiting for transfers between devices  8.2 us (4%)
  blocking collectives  7.73 us (4%)
  starting transfers between devices  7.69 us (4%)
  other arithmetic  2.98 us (2%)
  matrix products  2.11 us (1%)
  local copies, waits for them, and re-layouts  2.1 us (1%)
    pallas_call x2, Pallas kernels, rotation_of(): pl.pallas_call(rotation_kernel, out_shape=(jax.ShapeDtypeStruct((size, si...  97.5 us
    pallas_call x2, Pallas kernels, reduced_gram(): pl.pallas_call(functools.partial(reduce_kernel, count), out_shape=jax.Sha...  57.1 us
    ppermute x4, waiting for transfers between devices, from_behind(): lax.ppermute(value, axis, [(source, source + steps) for source in range(f...  8.2 us
    psum x1, blocking collectives, body(): totals = lax.psum(jnp.stack(coupling_terms), 'col')  7.73 us
    ppermute x4, starting transfers between devices, from_behind(): lax.ppermute(value, axis, [(source, source + steps) for source in range(f...  7.69 us
  transfers between devices with their start and end apart: 4, of which 2 were waited for; matrix products, arithmetic and copies ran while one was open for 1% of the time, Pallas kernels for 0%

profile of v2, /device:TPU:0, one launch (start us, length us, event | category | flops | bytes accessed | tf_op | source)
XLA Modules:
  0.0 186.2 jit_solution(16534732096537094895)
XLA Ops:
  0.6 0.0 copy-start
  0.6 1.0 copy-done
  1.7 29.1 %shard_map.30.gram_ref = f32[768,256]{1,0:T(8,128)S(1)} custom-call(f32[256,512]{1,0:T(8,128)S(1)} %copy-done), custom_call_target="tpu_custom_call" | custom-call | tf_op jit(solution)/shard_map/pallas_call | solution.py:235
  30.8 48.7 %shard_map.31 = (f32[512,512]{1,0:T(8,128)S(1)}, f32[8,128]{1,0:T(8,128)S(1)}) custom-call(f32[768,256]{1,0:T(8,128)S(1)} %shard_map.30.gram_ref), custom_call_target="tpu_custom_call" | custom-call | tf_op jit(solution)/shard_map/pallas_call | solution.py:140
  79.6 1.1 convolution_bitcast_fusion.1
  80.7 3.5 %collective-permute-start = (f32[256,256]{1,0:T(8,128)S(1)}, f32[256,256]{1,0:T(8,128)S(1)}, u32[]{:S(2)}, u32[]{:S(2)}) collective-permute-start(f32[256,256]{1,0:T(8,128)S(1)} %fusion.2), channel_id=1, source_target_pairs={{0,1},{2,3},{4,5},{6,7},{8,9},{10,11},{12,13},{14,15},{16,17},{18,... | collective-permute-start | bytes 786440 | tf_op jit(solution)/shard_map/ppermute | solution.py:16
  84.1 1.5 collective-permute-start.1
  85.6 0.5 slice.22
  86.1 4.0 %collective-permute-done = f32[256,256]{1,0:T(8,128)S(1)} collective-permute-done((f32[256,256]{1,0:T(8,128)S(1)}, f32[256,256]{1,0:T(8,128)S(1)}, u32[]{:S(2)}, u32[]{:S(2)}) %collective-permute-start) | collective-permute-done | bytes 262176 | tf_op jit(solution)/shard_map/ppermute | solution.py:16
  90.2 4.2 %collective-permute-done.1 = f32[256,256]{1,0:T(8,128)S(1)} collective-permute-done((f32[256,256]{1,0:T(8,128)S(1)}, f32[256,256]{1,0:T(8,128)S(1)}, u32[]{:S(2)}, u32[]{:S(2)}) %collective-permute-start.1) | collective-permute-done | bytes 262176 | tf_op jit(solution)/shard_map/ppermute | solution.py:16
  94.3 0.1 fusion.1
  94.4 0.1 pad_maximum_fusion.pair_ref
  94.5 28.0 %shard_map.32.gram_ref = f32[768,256]{1,0:T(8,128)S(1)} custom-call(f32[256,512]{1,0:T(8,128)S(1)} %pad_maximum_fusion.pair_ref), custom_call_target="tpu_custom_call" | custom-call | tf_op jit(solution)/shard_map/pallas_call | solution.py:235
  122.5 48.7 %shard_map.33 = (f32[512,512]{1,0:T(8,128)S(1)}, f32[8,128]{1,0:T(8,128)S(1)}) custom-call(f32[768,256]{1,0:T(8,128)S(1)} %shard_map.32.gram_ref), custom_call_target="tpu_custom_call" | custom-call | tf_op jit(solution)/shard_map/pallas_call | solution.py:140
  171.2 1.1 convolution_bitcast_fusion
  172.4 0.5 slice.23
  172.9 1.5 collective-permute-start.2
  174.4 1.3 collective-permute-start.3
  175.7 1.4 pad_maximum_fusion.2
  177.0 7.7 %psum.7 = f32[2]{0:T(128)S(1)} all-reduce(f32[2]{0:T(128)S(1)} %pad_maximum_fusion.2), channel_id=1, replica_groups=mesh['row'=16,'col'=2] {'col'}, use_global_device_ids=true, to_apply=%region_0.1 | all-reduce | flops 2 | bytes 16 | tf_op jit(solution)/shard_map/psum | solution.py:287
  184.8 0.5 multiply_sqrt_fusion
  185.3 0.0 collective-permute-done.2
  185.3 0.0 collective-permute-done.3
  185.3 0.1 fusion.4
  185.4 0.9 pad_maximum_fusion.1
  (4 shorter events, 0.1 us)
Async XLA Ops:
  0.6 1.0 copy-start
  80.7 9.5 %collective-permute-start = (f32[256,256]{1,0:T(8,128)S(1)}, f32[256,256]{1,0:T(8,128)S(1)}, u32[]{:S(2)}, u32[]{:S(2)}) collective-permute-start(f32[256,256]{1,0:T(8,128)S(1)} %fusion.2), channel_id=1, source_target_pairs={{0,1},{2,3},{4,5},{6,7},{8,9},{10,11},{12,13},{14,15},{16,17},{18,... | collective-permute-start | bytes 786440 | tf_op jit(solution)/shard_map/ppermute | solution.py:16
  84.1 10.2 %collective-permute-start.1 = (f32[256,256]{1,0:T(8,128)S(1)}, f32[256,256]{1,0:T(8,128)S(1)}, u32[]{:S(2)}, u32[]{:S(2)}) collective-permute-start(f32[256,256]{1,0:T(8,128)S(1)} %slice_bitcast_fusion.2), channel_id=1, source_target_pairs={{1,0},{3,2},{5,4},{7,6},{9,8},{11,10},{13,12},{15,14},{17,16},{19,... | collective-permute-start | bytes 786440 | tf_op jit(solution)/shard_map/ppermute | solution.py:16
  172.9 12.4 %collective-permute-start.2 = (f32[256,256]{1,0:T(8,128)S(1)}, f32[256,256]{1,0:T(8,128)S(1)}, u32[]{:S(2)}, u32[]{:S(2)}) collective-permute-start(f32[256,256]{1,0:T(8,128)S(1)} %fusion.5), channel_id=1, source_target_pairs={{0,1},{2,3},{4,5},{6,7},{8,9},{10,11},{12,13},{14,15},{16,17},{18,... | collective-permute-start | bytes 786440 | tf_op jit(solution)/shard_map/ppermute | solution.py:16
  174.4 10.9 %collective-permute-start.3 = (f32[256,256]{1,0:T(8,128)S(1)}, f32[256,256]{1,0:T(8,128)S(1)}, u32[]{:S(2)}, u32[]{:S(2)}) collective-permute-start(f32[256,256]{1,0:T(8,128)S(1)} %slice_bitcast_fusion), channel_id=1, source_target_pairs={{1,0},{3,2},{5,4},{7,6},{9,8},{11,10},{13,12},{15,14},{17,16},{19,... | collective-permute-start | bytes 786440 | tf_op jit(solution)/shard_map/ppermute | solution.py:16

commit v3 on v2

--- a/solution.py
+++ b/solution.py
@@ -8,12 +8,6 @@
 from jax.sharding import PartitionSpec as P
 
 STEPS = 2
-
-
-def from_behind(value, axis, steps):
-    count = lax.axis_size(axis)
-    first, last = (max(0, -steps), min(count, count - steps))
-    return lax.ppermute(value, axis, [(source, source + steps) for source in range(first, last)])
 
 
 LEAF = 128
@@ -152,7 +146,7 @@
         ],
         compiler_params=pltpu.CompilerParams(vmem_limit_bytes=32 << 20),
     )(pair_gram)
-    return turn, term[0, 0]
+    return turn, term
 
 
 def reduce_kernel(count, pair_ref, out_ref, mine, half_in, half, part_in, part, chunk_in, send, recv):
@@ -253,41 +247,117 @@
     )(pair)
 
 
+def turn_kernel(count, pair_ref, turn_ref, terms_ref, out_ref, total_ref, leaving, shares, send, recv):
+    width = pair_ref.shape[1] // 2
+    place = lax.axis_index("col")
+    last = count - 1
+    peers = [lax.rem(place + step, count) for step in range(1, count)]
+    left = pl.ds(0, width)
+    right = pl.ds(width, width)
+
+    barrier = pltpu.get_barrier_semaphore()
+    for peer in peers:
+        pl.semaphore_signal(
+            barrier, inc=1, device_id={"col": peer}, device_id_type=pl.DeviceIdType.MESH
+        )
+
+    def put(source, target, index, peer):
+        return pltpu.make_async_remote_copy(
+            src_ref=source,
+            dst_ref=target,
+            send_sem=send.at[index],
+            recv_sem=recv.at[index],
+            device_id={"col": peer},
+            device_id_type=pl.DeviceIdType.MESH,
+        )
+
+    leaving[1] = mat(pair_ref[...], turn_ref[width:, :], ((1,), (1,)))
+    pl.semaphore_wait(barrier, count - 1)
+    first_out = put(leaving.at[1], out_ref.at[:, left], 0, jnp.minimum(place + 1, last))
+    top_out = put(leaving.at[0], out_ref.at[:, left], 0, jnp.minimum(place + 1, last))
+    bottom_out = put(leaving.at[1], out_ref.at[:, right], 1, jnp.maximum(place - 1, 0))
+    spread_out = [
+        put(terms_ref, shares.at[place], 1 + step, peers[step - 1]) for step in range(1, count)
+    ]
+
+    @pl.when(place == 0)
+    def _():
+        first_out.start()
+
+    @pl.when(place > 0)
+    def _():
+        bottom_out.start()
+
+    for copy in spread_out:
+        copy.start()
+
+    leaving[0] = mat(pair_ref[...], turn_ref[:width, :], ((1,), (1,)))
+
+    @pl.when(jnp.logical_and(place > 0, place < last))
+    def _():
+        top_out.start()
+
+    @pl.when(place == 0)
+    def _():
+        out_ref[:, left] = leaving[0]
+
+    @pl.when(place == last)
+    def _():
+        out_ref[:, right] = leaving[0]
+
+    shares[place] = terms_ref[...]
+    for copy in spread_out:
+        copy.wait()
+    total = shares[0]
+    for step in range(1, count):
+        total += shares[step]
+    total_ref[...] = total
+
+    @pl.when(place < last)
+    def _():
+        top_out.wait_send()
+        bottom_out.wait_recv()
+
+    @pl.when(place > 0)
+    def _():
+        bottom_out.wait_send()
+        top_out.wait_recv()
+
+
+def turned_pair(pair, turn, terms):
+    width = pair.shape[1] // 2
+    count = lax.axis_size("col")
+    vmem = pl.BlockSpec(memory_space=pltpu.VMEM)
+    return pl.pallas_call(
+        functools.partial(turn_kernel, count),
+        out_shape=(
+            jax.ShapeDtypeStruct(pair.shape, jnp.float32),
+            jax.ShapeDtypeStruct(terms.shape, jnp.float32),
+        ),
+        in_specs=[vmem, vmem, vmem],
+        out_specs=(vmem, vmem),
+        scratch_shapes=[
+            pltpu.VMEM((2, pair.shape[0], width), jnp.float32),
+            pltpu.VMEM((count,) + terms.shape, jnp.float32),
+            pltpu.SemaphoreType.DMA((count + 1,)),
+            pltpu.SemaphoreType.DMA((count + 1,)),
+        ],
+        compiler_params=pltpu.CompilerParams(
+            collective_id=1, has_side_effects=True, vmem_limit_bytes=32 << 20
+        ),
+    )(pair, turn, terms)
+
+
 def body(matrix):
     width = matrix.shape[1] // 2
-    col_place = lax.axis_index("col")
-    col_last = lax.axis_size("col") - 1
-    first_col = col_place == 0
-    last_col = col_place == col_last
-    top_block = matrix[:, :width]
-    bottom_block = matrix[:, width:]
-    pair_blocks = matrix[None]
-    pair_gram = reduced_gram(pair_blocks[0])
-    coupling_terms = []
-    for step_index in range(STEPS):
-        turn, local_term = rotation_of(pair_gram)
-        coupling_terms.append(local_term)
-        turned = jnp.einsum(
-            "prk,lk->prl",
-            pair_blocks,
-            turn,
-            precision=lax.Precision.HIGHEST,
-            preferred_element_type=jnp.float32,
-        )
-        new_top = turned[0, :, :width]
-        new_bottom = turned[0, :, width:]
-        outgoing = jnp.where(first_col, new_bottom, new_top)
-        arrived_top = from_behind(outgoing, "col", 1)
-        arrived_bottom = from_behind(new_bottom, "col", -1)
-        top_block = jnp.where(first_col, new_top, arrived_top)
-        bottom_block = jnp.where(last_col, new_top, arrived_bottom)
-        pair_blocks = jnp.concatenate([top_block, bottom_block], axis=1)[None]
-        if step_index + 1 < STEPS:
-            pair_gram = reduced_gram(pair_blocks[0])
-    totals = lax.psum(jnp.stack(coupling_terms), "col")
-    coupling = jnp.sqrt(totals / (1.0 * lax.axis_size("col") * width))
-    rotated = jnp.concatenate([top_block, bottom_block], axis=1)
-    return (rotated, coupling)
+    pair = matrix
+    totals = []
+    for _ in range(STEPS):
+        turn, terms = rotation_of(reduced_gram(pair))
+        pair, total = turned_pair(pair, turn, terms)
+        totals.append(total[0, 0])
+    coupling = jnp.sqrt(jnp.stack(totals) / (1.0 * lax.axis_size("col") * width))
+    return (pair, coupling)
 
 
 def solution(mesh):

time: 186 us -> 178 us (0.957)
  Pallas kernels: 155 us -> 173 us
  waiting for transfers between devices: 8.2 us -> 0 us
  blocking collectives: 7.73 us -> 0 us
  starting transfers between devices: 7.69 us -> 0 us
  matrix products: 2.11 us -> 0 us
    pallas_call x0 -> x2, Pallas kernels: none -> 18.3 us  [turned_pair(): pl.pallas_call(functools.partial(turn_kernel, count), out_shape=(jax.Shap...]
    ppermute x4 -> x0, waiting for transfers between devices: 8.2 us -> none  [from_behind(): lax.ppermute(value, axis, [(source, source + steps) for source in range(f...]
    psum x1 -> x0, blocking collectives: 7.73 us -> none  [body(): totals = lax.psum(jnp.stack(coupling_terms), 'col')]
    ppermute x4 -> x0, starting transfers between devices: 7.69 us -> none  [from_behind(): lax.ppermute(value, axis, [(source, source + steps) for source in range(f...]
    dot_general x2 -> x0, matrix products: 2.11 us -> none  [body(): jnp.einsum('prk,lk->prl', pair_blocks, turn, precision=lax.Precision.HIGH...]
  transfers between devices with their start and end apart: 4 -> 0, of which waited for: 2 -> 0; matrix products, arithmetic and copies ran while one was open for 1% -> 0% of each run, Pallas kernels for 0% -> 0%
where the time goes in v3:
time: 178 us
  Pallas kernels  173 us (97%)
  local copies, waits for them, and re-layouts  2.86 us (2%)
  other arithmetic  1.85 us (1%)
    pallas_call x2, Pallas kernels, rotation_of(): pl.pallas_call(rotation_kernel, out_shape=(jax.ShapeDtypeStruct((size, si...  97.5 us
    pallas_call x2, Pallas kernels, reduced_gram(): pl.pallas_call(functools.partial(reduce_kernel, count), out_shape=jax.Sha...  57.1 us
    pallas_call x2, Pallas kernels, turned_pair(): pl.pallas_call(functools.partial(turn_kernel, count), out_shape=(jax.Shap...  18.3 us

profile of v3, /device:TPU:0, one launch (start us, length us, event | category | flops | bytes accessed | tf_op | source)
XLA Modules:
  0.0 178.3 jit_solution(14076761624785502426)
XLA Ops:
  0.6 0.0 copy-start
  0.6 1.0 copy-done
  1.7 29.1 %shard_map.30.gram_ref = f32[768,256]{1,0:T(8,128)S(1)} custom-call(f32[256,512]{1,0:T(8,128)S(1)} %copy-done), custom_call_target="tpu_custom_call" | custom-call | tf_op jit(solution)/shard_map/pallas_call | solution.py:229
  30.8 48.7 %shard_map.31 = (f32[512,512]{1,0:T(8,128)S(1)}, f32[8,128]{1,0:T(8,128)S(1)}) custom-call(f32[768,256]{1,0:T(8,128)S(1)} %shard_map.30.gram_ref), custom_call_target="tpu_custom_call" | custom-call | tf_op jit(solution)/shard_map/pallas_call | solution.py:134
  79.6 9.5 %shard_map.32 = (f32[256,512]{1,0:T(8,128)S(1)}, f32[8,128]{1,0:T(8,128)S(1)}) custom-call(f32[256,512]{1,0:T(8,128)S(1)} %copy-done, f32[512,512]{1,0:T(8,128)S(1)} %get-tuple-element.10.turn_ref, f32[8,128]{1,0:T(8,128)S(1)} %get-tuple-element.11.terms_ref), custom_call_target="tpu_custom_call" | custom-call | tf_op jit(solution)/shard_map/pallas_call | solution.py:331
  89.1 0.5 slice.6
  89.6 28.0 %shard_map.33.gram_ref = f32[768,256]{1,0:T(8,128)S(1)} custom-call(f32[256,512]{1,0:T(8,128)S(1)} %get-tuple-element.12.pair_ref), custom_call_target="tpu_custom_call" | custom-call | tf_op jit(solution)/shard_map/pallas_call | solution.py:229
  117.6 48.7 %shard_map.34 = (f32[512,512]{1,0:T(8,128)S(1)}, f32[8,128]{1,0:T(8,128)S(1)}) custom-call(f32[768,256]{1,0:T(8,128)S(1)} %shard_map.33.gram_ref), custom_call_target="tpu_custom_call" | custom-call | tf_op jit(solution)/shard_map/pallas_call | solution.py:134
  166.3 8.8 %shard_map.35 = (f32[256,512]{1,0:T(8,128)S(1)}, f32[8,128]{1,0:T(8,128)S(1)}) custom-call(f32[256,512]{1,0:T(8,128)S(1)} %get-tuple-element.12.pair_ref, f32[512,512]{1,0:T(8,128)S(1)} %get-tuple-element.13.turn_ref, f32[8,128]{1,0:T(8,128)S(1)} %get-tuple-element.14.terms_ref), custom_call_target="tpu_custom_call" | custom-call | tf_op jit(solution)/shard_map/pallas_call | solution.py:331
  175.1 0.5 slice.7
  175.6 1.9 %fusion = f32[2]{0:T(128)} fusion(f32[1]{0:T(128)} %bitcast.1, f32[1]{0:T(128)} %bitcast), kind=kLoop, calls=%fused_computation.1 | loop fusion | flops 4 | bytes 16 | tf_op jit(solution)/shard_map/sqrt | solution.py:359
  177.5 0.8 copy.4
Async XLA Ops:
  0.6 1.0 copy-start
